TPU v7x, 32 devices: a whole 2x2x4 slice. The times are simulated.
32 devices in a mesh: seq: 16 (over z, x, core), head: 2 (over y).
Axes of the slice: x: 2, y: 2, z: 4, core: 2. Of those that a mesh axis runs over, the one named last changes fastest.
Arguments:
- queries: bfloat16 [16384, 5120], P(('seq', 'head')), may hold values from -7.5 to 7.5
- keys: bfloat16 [16384, 1024], P(('seq', 'head')), may hold values from -7.5 to 7.5
- values: bfloat16 [16384, 1024], P(('seq', 'head')), may hold values from -6 to 6
- fetch_list: int32 [16, 16, 2], replicated, may hold values from 0 to 15, as said below
- choose: int32 [256, 16], P('seq'), may hold values from 0 to 31, as said below
- live: int32 [256], P('seq'), may hold values from 0 to 16, as said below
Outputs:
- attn_out: bfloat16 [16384, 5120], P(('seq', 'head'))
Inputs may be any that keep to these rules, and one draw needn't show every extreme that they name: Each row fetch_list[d, s] holds 2 distinct blocks. Each row of choose holds 16 distinct slots; slot j stands for entry j % 2 of fetch_list[d, j // 2]; the first live[b] entries of row b name slots j with j // 2 < b // 16. live[b] is at most 2 * (b // 16); every draw has a block with live equal to 16.
All inputs are finite; a program needn't handle non-finite values.
Results may differ from a plain program's by a relative error of at most 0.0042.
Values may be sent and summed in bfloat16 or wider, within the bound.
No kernel may reach another device: no remote copies, remote signals or barrier semaphores. Data moves between devices by JAX's collectives and lax.ppermute only.
A program may use at most 64 MiB of HBM per device.

v0:
```python
import functools
import math

import jax
import jax.numpy as jnp
from jax import lax
from jax.experimental import pallas as pl
from jax.experimental.pallas import tpu as pltpu
from jax.sharding import PartitionSpec as P

HEAD_WIDTH = 128
BLOCK_TOKENS = 64
LISTED_ENTRIES = 16
CAP = 2
STEP_BLOCKS = 4
MASKED = -1e30
NEAR = 4
ATTEND_FLOPS = 6 * 10**9
ROW_ORDER = (2, 1, 3)
PICK_FLOPS = 5 * 10**9
VMEM_BYTES = 63 * 2**20
ANY = pl.BlockSpec(memory_space=pl.ANY)
SMEM = pl.BlockSpec(memory_space=pltpu.SMEM)


def entries(rows_of):
    return [(a, m) for a in range(rows_of) for m in range(NEAR) if (a, m) != (0, 0)]


def count_of(form, rows_of):
    return {"shard": 1, "place": NEAR, "row": rows_of}[form]


def lengths_of(form, rows_of):
    if form == "place":
        return [rows_of - (m == 0) for m in range(NEAR)]
    return [NEAR - (a == 0) for a in range(rows_of)]


def entry_of(form, arrays, ahead, m):
    if form == "place":
        return arrays[m].at[ahead - (m == 0)]
    return arrays[ahead].at[m - (ahead == 0)]


def pick_kernel(shape, place, wanted, keys, values, *refs):
    planes, n_seq, forms, tokens, local_heads, first = shape
    rows_of, near = n_seq // NEAR, NEAR
    group_heads = len(forms)
    others, outs = refs[: planes - 1], refs[planes - 1 : -3]
    shard, load_sems, sems = refs[-3:]
    seq, head = place[0], place[1]
    lanes = group_heads * HEAD_WIDTH
    column = pl.multiple_of((head * local_heads + first) * HEAD_WIDTH, HEAD_WIDTH)

    def part(plane):
        return pl.ds(pl.multiple_of(plane * tokens, tokens), tokens)

    loads = []
    for which, source in enumerate((keys, values)):
        loads.append((source.at[:, pl.ds(column, lanes)], shard.at[which, part(head)]))
    for turn in range(1, planes):
        loads.append((others[turn - 1], shard.at[:, part(lax.rem(head + turn, planes))]))
    loads = [pltpu.make_async_copy(*ends, load_sems.at[i]) for i, ends in enumerate(loads)]
    for copy in loads:
        copy.start()
    for copy in loads:
        copy.wait()

    def each(h, dest, out, act):
        columns = slice(h * HEAD_WIDTH, (h + 1) * HEAD_WIDTH)
        for entry in range(CAP):
            row = pl.multiple_of(wanted[dest, entry] * BLOCK_TOKENS, BLOCK_TOKENS)
            source = shard.at[:, pl.ds(row, BLOCK_TOKENS), columns]
            into = out.at[:, pl.ds(entry * BLOCK_TOKENS, BLOCK_TOKENS)]
            act(pltpu.make_async_copy(source, into, sems.at[h, dest, entry]))

    def all_of(act):
        at = 0
        for h, form in enumerate(forms):
            mine = outs[at : at + count_of(form, rows_of)]
            at += len(mine)
            if form == "shard":

                @pl.loop(seq + 1, n_seq)
                def _(dest):
                    each(h, dest, mine[0].at[dest], act)

            else:
                for ahead, m in entries(rows_of):
                    dest = (seq // near + ahead) * near + jnp.bitwise_xor(seq % near, m)

                    @pl.when((dest > seq) & (dest < n_seq))
                    def _():
                        each(h, dest, entry_of(form, mine, ahead, m), act)

    all_of(lambda copy: copy.start())
    all_of(lambda copy: copy.wait())


def regroup_kernel(shape, place, *refs):
    n_seq, form, into, back, passed = shape
    rows_of = n_seq // NEAR
    n_in, n_out = count_of(form, rows_of), count_of(into, rows_of)
    ins, refs = refs[:n_in], refs[n_in + passed :]
    outs, bufs = refs[:n_out], refs[n_out + passed : -2]
    load_sems, sems = refs[-2:]
    row = place[0] // NEAR
    loads = [pltpu.make_async_copy(ins[i], bufs[i], load_sems.at[i]) for i in range(n_in)]

    def stores(act):
        for ahead, m in entries(rows_of):

            @pl.when((row - ahead >= 0) if back else (row + ahead < rows_of))
            def _():
                ends = entry_of(form, bufs, ahead, m), entry_of(into, outs, ahead, m)
                act(pltpu.make_async_copy(*ends, sems.at[ahead, m]))

    for copy in loads:
        copy.start()
    for copy in loads:
        copy.wait()
    stores(lambda copy: copy.start())
    stores(lambda copy: copy.wait())


def attend_scratch(n_seq, tokens, group_heads, repeat):
    blocks_here = tokens // BLOCK_TOKENS
    rows, columns = repeat * BLOCK_TOKENS, STEP_BLOCKS * BLOCK_TOKENS
    steps = LISTED_ENTRIES // STEP_BLOCKS + 1
    units = group_heads * blocks_here * steps + 5
    return [
        pltpu.VMEM((group_heads, tokens, repeat * HEAD_WIDTH), jnp.bfloat16),
        pltpu.VMEM(
            (group_heads, 2, (n_seq * CAP + blocks_here) * BLOCK_TOKENS, HEAD_WIDTH), jnp.bfloat16
        ),
        pltpu.VMEM((group_heads, tokens + BLOCK_TOKENS, repeat * HEAD_WIDTH), jnp.bfloat16),
        pltpu.VMEM((rows, columns), jnp.float32),
        pltpu.VMEM((rows, columns), jnp.float32),
        pltpu.VMEM((rows, columns), jnp.bfloat16),
        pltpu.VMEM((rows, columns), jnp.bfloat16),
        pltpu.VMEM((rows, HEAD_WIDTH), jnp.float32),
        pltpu.VMEM((rows, HEAD_WIDTH), jnp.float32),
        pltpu.VMEM((rows, HEAD_WIDTH), jnp.float32),
        pltpu.VMEM((rows, HEAD_WIDTH), jnp.float32),
        pltpu.SMEM((units, 5), jnp.int32),
        pltpu.SMEM((units, STEP_BLOCKS), jnp.int32),
        pltpu.SemaphoreType.DMA((group_heads, 3)),
        pltpu.SemaphoreType.DMA((n_seq, group_heads)),
        pltpu.SemaphoreType.DMA((group_heads, blocks_here)),
    ]


def attend_kernel(shape, place, choose, live, queries, keys, values, *refs):
    n_seq, n_head, local_heads, repeat, jobs, given, outs = shape
    group_heads = len(jobs)
    pieces = []
    for whose, plane, _, form in jobs:
        count = count_of(form, n_seq // NEAR)
        pieces.append((form, refs[:count] if form != "shard" else [refs[0].at[plane if whose == "plane" else 0]]))
        refs = refs[count:]
    out = refs[given]
    refs = refs[given + outs :]
    q_buf, kv_buf, o_buf = refs[:3]
    scores, weights = refs[3:5], refs[5:7]
    acc, top, total, shrink, units, taken, sems, piece_sems, out_sems = refs[7:]
    tokens = q_buf.shape[1]
    blocks_here = tokens // BLOCK_TOKENS
    seq, head = place[0], place[1]
    first_block = head * blocks_here
    slots = n_seq * CAP
    q_lanes = repeat * HEAD_WIDTH
    piece_rows = CAP * BLOCK_TOKENS
    own_rows = pl.ds(slots * BLOCK_TOKENS, tokens)
    columns = STEP_BLOCKS * BLOCK_TOKENS
    rows = repeat * BLOCK_TOKENS

    def kv_head(h):
        whose, plane, at, _ = jobs[h]
        return (lax.rem(head + plane, n_head) if whose == "turn" else plane) * local_heads + at

    q_heads = [kv_head(h) for h in range(group_heads)]

    loads = []
    for h in range(group_heads):
        q_cols = pl.ds(pl.multiple_of(q_heads[h] * q_lanes, HEAD_WIDTH), q_lanes)
        kv_cols = pl.ds(pl.multiple_of(q_heads[h] * HEAD_WIDTH, HEAD_WIDTH), HEAD_WIDTH)
        loads += [
            pltpu.make_async_copy(queries.at[:, q_cols], q_buf.at[h], sems.at[h, 0]),
            pltpu.make_async_copy(keys.at[:, kv_cols], kv_buf.at[h, 0, own_rows], sems.at[h, 1]),
            pltpu.make_async_copy(values.at[:, kv_cols], kv_buf.at[h, 1, own_rows], sems.at[h, 2]),
        ]

    def piece_do(h, source, piece, act):
        into = pl.ds(pl.multiple_of(source * piece_rows, piece_rows), piece_rows)
        act(pltpu.make_async_copy(piece, kv_buf.at[h, :, into], piece_sems.at[source, h]))

    def pieces_do(act):
        for h, (form, arrays) in enumerate(pieces):
            if form == "shard":

                @pl.loop(0, seq)
                def _(source):
                    piece_do(h, source, arrays[0].at[source], act)

            else:
                for behind, m in entries(n_seq // NEAR):
                    source = (seq // NEAR - behind) * NEAR + jnp.bitwise_xor(seq % NEAR, m)

                    @pl.when((source >= 0) & (source < seq))
                    def _():
                        piece_do(h, source, entry_of(form, arrays, behind, m), act)

    for copy in loads:
        copy.start()
    pieces_do(lambda copy: copy.start())

    def put(unit, h, block, at, last, out_block):
        units[unit, 0] = h
        units[unit, 1] = block
        units[unit, 2] = at
        units[unit, 3] = last
        units[unit, 4] = out_block
        count = live[first_block + block]
        for i in range(STEP_BLOCKS):
            entry = at * STEP_BLOCKS + i
            slot = choose[first_block + block, jnp.clip(entry - 1, 0, LISTED_ENTRIES - 1)]
            dead = (entry == 0) | (entry > count)
            taken[unit, i] = jnp.where(dead, slots + block, slot) * BLOCK_TOKENS

    for fill in range(2):
        put(fill, 0, 0, 0, 0, blocks_here)

    def put_block(i, at_unit):
        h, block = i // blocks_here, i % blocks_here
        steps = (live[first_block + block] + STEP_BLOCKS) // STEP_BLOCKS

        @pl.loop(0, steps)
        def _(at):
            put(at_unit + at, h, block, at, jnp.where(at == steps - 1, 1, 0), block)

        return at_unit + steps

    last_unit = lax.fori_loop(0, group_heads * blocks_here, put_block, jnp.int32(2))
    for fill in range(3):
        put(last_unit + fill, 0, 0, 0, 0, blocks_here)

    for buf in (*scores, *weights, acc, top, total, shrink):
        buf[...] = jnp.zeros_like(buf)

    for copy in loads:
        copy.wait()
    pieces_do(lambda copy: copy.wait())

    factor = math.log2(math.e) / math.sqrt(HEAD_WIDTH)
    column = lax.broadcasted_iota(jnp.int32, (BLOCK_TOKENS, columns), 1)
    row = lax.broadcasted_iota(jnp.int32, (BLOCK_TOKENS, columns), 0)

    def block_rows(block):
        return pl.ds(pl.multiple_of(block * BLOCK_TOKENS, BLOCK_TOKENS), BLOCK_TOKENS)

    def out_copy(h, block):
        at = block_rows(block)
        q_head = q_heads[0]
        for i in range(1, group_heads):
            q_head = jnp.where(h == i, q_heads[i], q_head)
        q_cols = pl.ds(pl.multiple_of(q_head * q_lanes, HEAD_WIDTH), q_lanes)
        return pltpu.make_async_copy(o_buf.at[h, at], out.at[at, q_cols], out_sems.at[h, block])

    def gathered(unit, which):
        h = units[unit, 0]
        parts = []
        for i in range(STEP_BLOCKS):
            at = pl.ds(pl.multiple_of(taken[unit, i], BLOCK_TOKENS), BLOCK_TOKENS)
            parts.append(kv_buf[h, which, at, :])
        return jnp.concatenate(parts, axis=0)

    def turn(unit, now):
        oldest = unit - 2
        mixed = jnp.dot(weights[now][...], gathered(oldest, 1), preferred_element_type=jnp.float32)
        mixed = acc[...] * shrink[...] + mixed
        acc[...] = mixed
        result = (mixed * (1.0 / total[...])).astype(jnp.bfloat16)
        h, at = units[oldest, 0], block_rows(units[oldest, 4])
        for r in range(repeat):
            o_buf[h, at, r * HEAD_WIDTH : (r + 1) * HEAD_WIDTH] = result[
                r * BLOCK_TOKENS : (r + 1) * BLOCK_TOKENS
            ]

        before = unit - 1
        at_step = units[before, 2]
        count = live[first_block + units[before, 1]]
        limit = (count + 1 - at_step * STEP_BLOCKS) * BLOCK_TOKENS
        reach = jnp.where(at_step == 0, 0, columns)
        allowed = (column < limit) & ((column >= BLOCK_TOKENS) | (column <= row + reach))
        old = jnp.where(at_step == 0, MASKED, top[...])
        kept = jnp.where(
            allowed[None], scores[1 - now][...].reshape(repeat, BLOCK_TOKENS, columns), MASKED
        ).reshape(rows, columns)
        high = jnp.maximum(jnp.max(kept, axis=-1, keepdims=True), old)
        fade = jnp.exp2((old - high) * factor)
        parts = [
            jnp.exp2((kept[:, i : i + HEAD_WIDTH] - high) * factor)
            for i in range(0, columns, HEAD_WIDTH)
        ]
        sums = jnp.sum(functools.reduce(jnp.add, parts), axis=-1, keepdims=True)
        for i, part in enumerate(parts):
            weights[1 - now][:, i * HEAD_WIDTH : (i + 1) * HEAD_WIDTH] = part.astype(jnp.bfloat16)
        top[...] = high
        shrink[...] = fade
        total[...] = total[...] * fade + sums

        h, at = units[unit, 0], block_rows(units[unit, 1])
        q = jnp.concatenate(
            [q_buf[h, at, r * HEAD_WIDTH : (r + 1) * HEAD_WIDTH] for r in range(repeat)], axis=0
        )
        scores[now][...] = lax.dot_general(
            q, gathered(unit, 0), (((1,), (1,)), ((), ())), preferred_element_type=jnp.float32
        )

    def send(unit):
        @pl.when(units[unit, 3] == 1)
        def _():
            out_copy(units[unit, 0], units[unit, 1]).start()

    def two_turns(i, carry):
        unit = 2 * i
        turn(unit, 0)
        turn(unit + 1, 1)
        send(unit - 2)
        send(unit - 1)
        return carry

    lax.fori_loop(1, (last_unit + 3) // 2, two_turns, 0)

    for h in range(group_heads):

        @pl.loop(0, blocks_here)
        def _(block):
            out_copy(h, block).wait()


def body(queries, keys, values, fetch_list, choose, live, *, n_seq, n_head):
    tokens, q_width = queries.shape
    kv_heads = keys.shape[1] // HEAD_WIDTH
    repeat = q_width // HEAD_WIDTH // kv_heads
    local_heads = kv_heads // n_head
    rows_of = n_seq // NEAR
    seq, head = lax.axis_index("seq"), lax.axis_index("head")
    wanted = lax.dynamic_index_in_dim(fetch_list, seq, 1, keepdims=False)
    place = jnp.stack([seq, head]).astype(jnp.int32)

    def piece(*lead):
        return jax.ShapeDtypeStruct(lead + (2, CAP * BLOCK_TOKENS, HEAD_WIDTH), jnp.bfloat16)

    def exchange(first, heads):
        others = []
        for turn in range(1, n_head):
            theirs = lax.rem(head + n_head - turn, n_head) * local_heads + first
            part = jnp.stack(
                [
                    lax.dynamic_slice_in_dim(x, theirs * HEAD_WIDTH, heads * HEAD_WIDTH, axis=1)
                    for x in (keys, values)
                ]
            )
            back = [(h, (h + n_head - turn) % n_head) for h in range(n_head)]
            with jax.named_scope(f"other_plane_{first}"):
                others.append(lax.ppermute(part, "head", back))
        return others

    def pick(first, forms, others):
        shapes = []
        for form in forms:
            lengths = [n_seq] if form == "shard" else lengths_of(form, rows_of)
            shapes += [piece(n) for n in lengths]
        heads = len(forms)
        outs = list(
            pl.pallas_call(
                functools.partial(pick_kernel, (n_head, n_seq, forms, tokens, local_heads, first)),
                out_shape=shapes,
                in_specs=[SMEM, SMEM] + [ANY] * (2 + len(others)),
                out_specs=[ANY] * len(shapes),
                scratch_shapes=[
                    pltpu.VMEM((2, n_head * tokens, heads * HEAD_WIDTH), jnp.bfloat16),
                    pltpu.SemaphoreType.DMA((1 + n_head,)),
                    pltpu.SemaphoreType.DMA((heads, n_seq, CAP)),
                ],
                compiler_params=pltpu.CompilerParams(vmem_limit_bytes=VMEM_BYTES),
                cost_estimate=pl.CostEstimate(
                    flops=PICK_FLOPS * heads, bytes_accessed=2**20, transcendentals=0
                ),
                name="pick",
            )(place, wanted, keys, values, *others)
        )
        return [[outs.pop(0) for _ in range(count_of(form, rows_of))] for form in forms]

    def regroup(form, into, back, parts, *passed):
        n_in, n_out = len(parts), count_of(into, rows_of)
        shapes = [piece(n) for n in lengths_of(into, rows_of)]
        outs = pl.pallas_call(
            functools.partial(regroup_kernel, (n_seq, form, into, back, len(passed))),
            out_shape=shapes + [jax.ShapeDtypeStruct(x.shape, x.dtype) for x in passed],
            in_specs=[SMEM] + [ANY] * (n_in + len(passed)),
            out_specs=[ANY] * (n_out + len(passed)),
            scratch_shapes=[pltpu.VMEM(part.shape, part.dtype) for part in parts]
            + [pltpu.SemaphoreType.DMA((n_in,)), pltpu.SemaphoreType.DMA((rows_of, NEAR))],
            input_output_aliases={1 + n_in + i: n_out + i for i in range(len(passed))},
            compiler_params=pltpu.CompilerParams(vmem_limit_bytes=VMEM_BYTES),
            name="regroup",
        )(place, *parts, *passed)
        return list(outs[:n_out]), *outs[n_out:]

    def attend(jobs, *passed):
        operands = [place, choose, live, queries, keys, values]
        shapes = []
        for whose, plane, at, form, arrays in jobs:
            operands += arrays
            shapes.append((whose, plane, at, form))
        n = len(operands)
        outs = [queries if x is None else x for x in passed or [None]]
        given = [i for i, x in enumerate(outs) if passed and passed[i] is not None]
        operands += [passed[i] for i in given]
        return pl.pallas_call(
            functools.partial(
                attend_kernel, (n_seq, n_head, local_heads, repeat, tuple(shapes), len(given), len(outs))
            ),
            out_shape=[jax.ShapeDtypeStruct(x.shape, x.dtype) for x in outs],
            in_specs=[SMEM] * 3 + [ANY] * (len(operands) - 3),
            out_specs=[ANY] * len(outs),
            scratch_shapes=attend_scratch(n_seq, tokens, len(jobs), repeat),
            input_output_aliases={n + i: at for i, at in enumerate(given)},
            compiler_params=pltpu.CompilerParams(vmem_limit_bytes=VMEM_BYTES),
            cost_estimate=pl.CostEstimate(
                flops=ATTEND_FLOPS * len(jobs), bytes_accessed=2**20, transcendentals=0
            ),
            name="attend",
        )(*operands)

    def over_rows(arrays, at):
        got = [arrays[0]] + [None] * (rows_of - 1)
        for ahead in ROW_ORDER:
            if arrays[ahead] is None:
                continue
            step = ahead * NEAR
            pairs = [(s, s + step) for s in range(n_seq - step)]
            with jax.named_scope(f"row_{at}_{ahead}"):
                got[ahead] = lax.ppermute(arrays[ahead], "seq", pairs)
        return got

    def in_row(arrays, at):
        got = [arrays[0]]
        for m in range(1, NEAR):
            with jax.named_scope(f"place_{at}_{m}"):
                got.append(lax.ppermute(arrays[m], "seq", [(s, s ^ m) for s in range(n_seq)]))
        return got

    def swap(arrays, at):
        got = []
        for i, array in enumerate(arrays):
            with jax.named_scope(f"swap_{at}_{i}"):
                got.append(lax.ppermute(array, "head", [(0, 1), (1, 0)]))
        return got

    if n_head != 2 or rows_of != 4 or local_heads != 4:
        passed = []
        for at in range(local_heads):
            ((sends,),) = pick(at, ("shard",), exchange(at, 1))
            got = lax.all_to_all(sends, "seq", split_axis=0, concat_axis=0, tiled=True)
            whole = lax.all_gather(got, "head", axis=0, tiled=False)
            for plane in range(n_head):
                passed = attend([("plane", plane, at, "shard", [whole])], *passed)
        return passed[0]

    def direct(at, sends):
        with jax.named_scope(f"shard_{at}"):
            got = lax.all_to_all(sends, "seq", split_axis=0, concat_axis=0, tiled=True)
        return "shard", [got[None]]

    def own(at, imports):
        return ("turn", 0, at) + imports

    def turned(at, imports):
        form, arrays = imports
        return ("turn", 1, at, form, swap(arrays, at))

    others, rest = exchange(0, 1), exchange(1, 3)
    first = direct(0, pick(0, ("shard",), others)[0][0])
    (sends,), (third,), parts = pick(1, ("shard", "shard", "place"), rest)
    second = direct(1, sends)
    first_turned = swap(first[1], 0)
    out, straight = attend([own(0, first)], None, parts[0])
    parts = [straight] + in_row(parts, 3)[1:]
    grouped, third, *first_turned = regroup("place", "row", False, parts, third, *first_turned)
    third = direct(2, third)
    job = ("turn", 1, 0, "shard", first_turned)
    out, *grouped[:-1] = attend([job, own(1, second)], out, *grouped[:-1])
    ends = [(i, i ^ 1) for i in range(NEAR * n_head)]
    with jax.named_scope("swap_far"):
        twin = lax.ppermute(grouped[-1], ("seq", "head"), ends)
    out, grouped[-1], twin = attend([turned(1, second), own(2, third)], out, grouped[-1], twin)
    fourth = over_rows(grouped, 3)
    twin = over_rows([None] * (rows_of - 1) + [twin], 4)[-1]
    (out,) = attend([turned(2, third), own(3, ("row", fourth))], out)
    (out,) = attend([("turn", 1, 3, "row", swap(fourth[:-1], 3) + [twin])], out)
    return out


def solution(mesh):
    placed = (
        P(("seq", "head"), None),
        P(("seq", "head"), None),
        P(("seq", "head"), None),
        P(),
        P("seq", None),
        P("seq"),
    )
    return jax.shard_map(
        functools.partial(body, n_seq=mesh.shape["seq"], n_head=mesh.shape["head"]),
        mesh=mesh,
        in_specs=placed,
        out_specs=P(("seq", "head"), None),
        check_vma=False,
    )
```

profile of v0, /device:TPU:0, one launch (start us, length us, event | category | flops | bytes accessed | tf_op | source)
XLA Modules:
  0.0 159.3 jit_solution(4069141990045086103)
XLA Ops:
  0.0 1.0 dynamic-slice_bitcast_fusion.2
  1.0 3.0 %collective-permute-start = (bf16[2,512,128]{2,1,0:T(8,128)(2,1)S(1)}, bf16[2,512,128]{2,1,0:T(8,128)(2,1)}, u32[]{:S(2)}, u32[]{:S(2)}) collective-permute-start(bf16[2,512,128]{2,1,0:T(8,128)(2,1)S(1)} %pad_maximum_fusion.1), channel_id=1, source_target_pairs={{0,1},{1,0},{2,3},{3,2},{4,5},{5,4},{6,7},{7,6},{8,9},{9,8},{10,11... | collective-permute-start | bytes 786440 | tf_op jit(solution)/shard_map/other_plane_0/ppermute | solution.py:368
  4.1 1.2 dynamic-slice_bitcast_fusion
  5.3 0.1 pad_maximum_fusion
  5.4 0.1 collective-permute-start.1
  5.5 0.1 constant_dynamic-slice_fusion
  5.6 0.1 copy.19
  5.6 0.7 copy.20.wanted
  6.3 0.6 pad_add_fusion.place
  6.9 4.4 %collective-permute-done.refs_0_ = bf16[2,512,128]{2,1,0:T(8,128)(2,1)} collective-permute-done((bf16[2,512,128]{2,1,0:T(8,128)(2,1)S(1)}, bf16[2,512,128]{2,1,0:T(8,128)(2,1)}, u32[]{:S(2)}, u32[]{:S(2)}) %collective-permute-start) | collective-permute-done | bytes 262176 | tf_op jit(solution)/shard_map/other_plane_0/ppermute | solution.py:368
  11.3 3.1 %pick.2 = bf16[16,2,128,128]{3,2,1,0:T(8,128)(2,1)} custom-call(s32[2]{0:T(128)} %pad_add_fusion.place, s32[16,2]{1,0:T(8,128)} %copy.20.wanted, bf16[512,1024]{1,0:T(8,128)(2,1)} %keys.13, bf16[512,1024]{1,0:T(8,128)(2,1)} %values.13, bf16[2,512,128]{2,1,0:T(8,128)(2,1)} %collective-permute-done.refs_0_), custom_call_target="tpu_custom_call" | custom-call | flops 5000000000 | bytes 1048576 | tf_op jit(solution)/shard_map/pick/pallas_call | solution.py:378
  14.5 6.2 %all-to-all-start = ((bf16[16,2,128,128]{3,2,1,0:T(8,128)(2,1)}), bf16[16,2,128,128]{3,2,1,0:T(8,128)(2,1)}, u32[]{:S(2)}, u32[]{:S(2)}) async-start(bf16[16,2,128,128]{3,2,1,0:T(8,128)(2,1)} %pick.2), calls=%async_computation | async-start | bytes 2097152 | tf_op jit(solution)/shard_map/shard_0/all_to_all | solution.py:476
  20.7 6.7 %collective-permute-done.1.refs_0_ = bf16[2,512,384]{2,1,0:T(8,128)(2,1)} collective-permute-done((bf16[2,512,384]{2,1,0:T(8,128)(2,1)S(1)}, bf16[2,512,384]{2,1,0:T(8,128)(2,1)}, u32[]{:S(2)}, u32[]{:S(2)}) %collective-permute-start.1) | collective-permute-done | bytes 786464 | tf_op jit(solution)/shard_map/other_plane_1/ppermute | solution.py:368
  27.3 4.7 %pick.3 = (bf16[16,2,128,128]{3,2,1,0:T(8,128)(2,1)}, bf16[16,2,128,128]{3,2,1,0:T(8,128)(2,1)}, bf16[3,2,128,128]{3,2,1,0:T(8,128)(2,1)}, bf16[4,2,128,128]{3,2...) custom-call(s32[2]{0:T(128)} %pad_add_fusion.place, s32[16,2]{1,0:T(8,128)} %copy.20.wanted, ...), custom_call_target="tpu_custom_call" | custom-call | flops 15000000512 | bytes 1048576 | tf_op jit(solution)/shard_map/pick/pallas_call | solution.py:378
  32.0 11.7 %all-to-all-done = bf16[16,2,128,128]{3,2,1,0:T(8,128)(2,1)} async-done(((bf16[16,2,128,128]{3,2,1,0:T(8,128)(2,1)}), bf16[16,2,128,128]{3,2,1,0:T(8,128)(2,1)}, u32[]{:S(2)}, u32[]{:S(2)}) %all-to-all-start) | async-done | bytes 1048608 | tf_op jit(solution)/shard_map/shard_0/all_to_all | solution.py:476
  43.7 6.9 %all-to-all-start.1 = ((bf16[16,2,128,128]{3,2,1,0:T(8,128)(2,1)}), bf16[16,2,128,128]{3,2,1,0:T(8,128)(2,1)}, u32[]{:S(2)}, u32[]{:S(2)}) async-start(bf16[16,2,128,128]{3,2,1,0:T(8,128)(2,1)} %get-tuple-element.33), calls=%async_computation.1 | async-start | bytes 2097152 | tf_op jit(solution)/shard_map/shard_1/all_to_all | solution.py:476
  50.6 1.6 collective-permute-start.5
  52.2 0.0 collective-permute-start.2
  52.2 1.8 %collective-permute-start.3 = (bf16[4,2,128,128]{3,2,1,0:T(8,128)(2,1)}, bf16[4,2,128,128]{3,2,1,0:T(8,128)(2,1)S(1)}, u32[]{:S(2)}, u32[]{:S(2)}) collective-permute-start(bf16[4,2,128,128]{3,2,1,0:T(8,128)(2,1)} %get-tuple-element.29), channel_id=1, source_target_pairs={{0,4},{2,6},{4,0},{6,2},{8,12},{10,14},{12,8},{14,10},{16,20},{18,... | collective-permute-start | bytes 786440 | tf_op jit(solution)/shard_map/place_3_2/ppermute | solution.py:454
  54.0 0.1 collective-permute-start.4
  54.1 5.1 %attend.5 = (bf16[512,5120]{1,0:T(8,128)(2,1)}, bf16[3,2,128,128]{3,2,1,0:T(8,128)(2,1)}) custom-call(s32[2]{0:T(128)} %pad_add_fusion.place, s32[16,16]{1,0:T(8,128)} %choose.9, s32[16]{0:T(128)} %live.9, bf16[512,5120]{1,0:T(8,128)(2,1)} %queries.9, bf16[512,1024]{1,0:T(8,128)(2,1)} %keys.13, ...), custom_call_target="tpu_custom_call", output_to_operand_aliasing={{1}: (7, {})} | custom-call | flops 6000000000 | bytes 1048576 | tf_op jit(solution)/shard_map/attend/pallas_call | solution.py:423
  59.3 0.0 collective-permute-done.2.refs_1_
  59.3 8.9 %collective-permute-done.3.refs_2_ = bf16[4,2,128,128]{3,2,1,0:T(8,128)(2,1)S(1)} collective-permute-done((bf16[4,2,128,128]{3,2,1,0:T(8,128)(2,1)}, bf16[4,2,128,128]{3,2,1,0:T(8,128)(2,1)S(1)}, u32[]{:S(2)}, u32[]{:S(2)}) %collective-permute-start.3) | collective-permute-done | bytes 262176 | tf_op jit(solution)/shard_map/place_3_2/ppermute | solution.py:454
  68.2 7.5 %collective-permute-done.4.refs_3_ = bf16[4,2,128,128]{3,2,1,0:T(8,128)(2,1)S(1)} collective-permute-done((bf16[4,2,128,128]{3,2,1,0:T(8,128)(2,1)}, bf16[4,2,128,128]{3,2,1,0:T(8,128)(2,1)S(1)}, u32[]{:S(2)}, u32[]{:S(2)}) %collective-permute-start.4) | collective-permute-done | bytes 262176 | tf_op jit(solution)/shard_map/place_3_3/ppermute | solution.py:454
  75.7 0.7 collective-permute-done.5.refs_5_
  76.3 0.0 copy-done.3
  76.4 3.0 %regroup.1 = (bf16[3,2,128,128]{3,2,1,0:T(8,128)(2,1)}, bf16[4,2,128,128]{3,2,1,0:T(8,128)(2,1)}, bf16[4,2,128,128]{3,2,1,0:T(8,128)(2,1)}, bf16[4,2,128,128]{3,...) custom-call(s32[2]{0:T(128)} %pad_add_fusion.place, ...), custom_call_target="tpu_custom_call", output_to_operand_aliasing={{4}: (5, {}), {5}: (6, {})} | custom-call | tf_op jit(solution)/shard_map/regroup/pallas_call | solution.py:400
  79.4 5.5 %all-to-all-start.2 = ((bf16[16,2,128,128]{3,2,1,0:T(8,128)(2,1)}), bf16[16,2,128,128]{3,2,1,0:T(8,128)(2,1)}, u32[]{:S(2)}, u32[]{:S(2)}) async-start(bf16[16,2,128,128]{3,2,1,0:T(8,128)(2,1)} %get-tuple-element.41), calls=%async_computation.2 | async-start | bytes 2097152 | tf_op jit(solution)/shard_map/shard_2/all_to_all | solution.py:476
  84.9 1.6 collective-permute-start.11
  86.5 2.4 %collective-permute-start.12 = (bf16[4,2,128,128]{3,2,1,0:T(8,128)(2,1)}, bf16[4,2,128,128]{3,2,1,0:T(8,128)(2,1)S(1)}, u32[]{:S(2)}, u32[]{:S(2)}) collective-permute-start(bf16[4,2,128,128]{3,2,1,0:T(8,128)(2,1)} %get-tuple-element.43.refs_3_), channel_id=1, source_target_pairs={{0,1},{1,0},{2,3},{3,2},{4,5},{5,4},{6,7},{7,6}} | collective-permute-start | bytes 786440 | tf_op jit(solution)/shard_map/swap_far/ppermute | solution.py:499
  88.9 7.5 %attend.6 = (bf16[512,5120]{1,0:T(8,128)(2,1)}, bf16[3,2,128,128]{3,2,1,0:T(8,128)(2,1)}, bf16[4,2,128,128]{3,2,1,0:T(8,128)(2,1)}, bf16[4,2,128,128]{3,2,1,0:T(8,128)(2,1)}) custom-call(s32[2]{0:T(128)} %pad_add_fusion.place, s32[16,16]{1,0:T(8,128)} %choose.9, s32[16]{0:T(128)} %live.9, ...), custom_call_target="tpu_custom_call", output_to_operand_aliasing={{0}: (8, {}), {1}: (9, {}), {2}: (10, {}), {3}: (11, {})} | custom-call | flops 12000000000 | bytes 1048576 | tf_op jit(solution)/shard_map/attend/pallas_call | solution.py:423
  96.4 3.0 %collective-permute-start.7 = (bf16[4,2,128,128]{3,2,1,0:T(8,128)(2,1)}, bf16[4,2,128,128]{3,2,1,0:T(8,128)(2,1)S(1)}, u32[]{:S(2)}, u32[]{:S(2)}) collective-permute-start(bf16[4,2,128,128]{3,2,1,0:T(8,128)(2,1)} %get-tuple-element.39), channel_id=1, source_target_pairs={{0,8},{2,10},{4,12},{6,14},{8,16},{10,18},{12,20},{14,22},{16,24},... | collective-permute-start | bytes 786440 | tf_op jit(solution)/shard_map/row_3_1/ppermute | solution.py:447
  99.5 4.4 %collective-permute-start.9 = (bf16[4,2,128,128]{3,2,1,0:T(8,128)(2,1)}, bf16[4,2,128,128]{3,2,1,0:T(8,128)(2,1)S(1)}, u32[]{:S(2)}, u32[]{:S(2)}) collective-permute-start(bf16[4,2,128,128]{3,2,1,0:T(8,128)(2,1)} %get-tuple-element.40), channel_id=1, source_target_pairs={{0,16},{2,18},{4,20},{6,22},{8,24},{10,26},{12,28},{14,30},{1,17},... | collective-permute-start | bytes 786440 | tf_op jit(solution)/shard_map/row_3_2/ppermute | solution.py:447
  103.9 4.0 %all-to-all-done.2 = bf16[16,2,128,128]{3,2,1,0:T(8,128)(2,1)} async-done(((bf16[16,2,128,128]{3,2,1,0:T(8,128)(2,1)}), bf16[16,2,128,128]{3,2,1,0:T(8,128)(2,1)}, u32[]{:S(2)}, u32[]{:S(2)}) %all-to-all-start.2) | async-done | bytes 1048608 | tf_op jit(solution)/shard_map/shard_2/all_to_all | solution.py:476
  107.9 1.5 collective-permute-start.14
  109.4 7.4 %collective-permute-done.12.refs_4_ = bf16[4,2,128,128]{3,2,1,0:T(8,128)(2,1)S(1)} collective-permute-done((bf16[4,2,128,128]{3,2,1,0:T(8,128)(2,1)}, bf16[4,2,128,128]{3,2,1,0:T(8,128)(2,1)S(1)}, u32[]{:S(2)}, u32[]{:S(2)}) %collective-permute-start.12) | collective-permute-done | bytes 262176 | tf_op jit(solution)/shard_map/swap_far/ppermute | solution.py:499
  116.8 0.7 copy-done.7
  117.5 7.5 %attend.7 = (bf16[512,5120]{1,0:T(8,128)(2,1)}, bf16[4,2,128,128]{3,2,1,0:T(8,128)(2,1)}, bf16[4,2,128,128]{3,2,1,0:T(8,128)(2,1)}) custom-call(s32[2]{0:T(128)} %pad_add_fusion.place, s32[16,16]{1,0:T(8,128)} %choose.9, s32[16]{0:T(128)} %live.9, bf16[512,5120]{1,0:T(8,128)(2,1)} %queries.9, ...), custom_call_target="tpu_custom_call", output_to_operand_aliasing={{0}: (8, {}), {1}: (9, {}), {2}: (10, {})} | custom-call | flops 12000000000 | bytes 1048576 | tf_op jit(solution)/shard_map/attend/pallas_call | solution.py:423
  125.0 2.0 %collective-permute-start.15 = (bf16[4,2,128,128]{3,2,1,0:T(8,128)(2,1)}, bf16[4,2,128,128]{3,2,1,0:T(8,128)(2,1)}, u32[]{:S(2)}, u32[]{:S(2)}) collective-permute-start(bf16[4,2,128,128]{3,2,1,0:T(8,128)(2,1)} %get-tuple-element.45), channel_id=1, source_target_pairs={{0,24},{2,26},{4,28},{6,30},{1,25},{3,27},{5,29},{7,31}} | collective-permute-start | bytes 786440 | tf_op jit(solution)/shard_map/row_3_3/ppermute | solution.py:447
  127.0 1.5 collective-permute-start.6
  128.6 0.5 collective-permute-start.10
  129.1 1.5 collective-permute-start.8
  130.6 2.6 %collective-permute-done.15.refs_4_ = bf16[4,2,128,128]{3,2,1,0:T(8,128)(2,1)} collective-permute-done((bf16[4,2,128,128]{3,2,1,0:T(8,128)(2,1)}, bf16[4,2,128,128]{3,2,1,0:T(8,128)(2,1)}, u32[]{:S(2)}, u32[]{:S(2)}) %collective-permute-start.15) | collective-permute-done | bytes 262176 | tf_op jit(solution)/shard_map/row_3_3/ppermute | solution.py:447
  133.2 6.9 %collective-permute-start.13 = (bf16[4,2,128,128]{3,2,1,0:T(8,128)(2,1)}, bf16[4,2,128,128]{3,2,1,0:T(8,128)(2,1)}, u32[]{:S(2)}, u32[]{:S(2)}) collective-permute-start(bf16[4,2,128,128]{3,2,1,0:T(8,128)(2,1)} %get-tuple-element.44), channel_id=1, source_target_pairs={{0,24},{2,26},{4,28},{6,30},{1,25},{3,27},{5,29},{7,31}} | collective-permute-start | bytes 786440 | tf_op jit(solution)/shard_map/row_4_3/ppermute | solution.py:447
  140.1 7.6 %attend.8.refs_4_ = bf16[512,5120]{1,0:T(8,128)(2,1)} custom-call(s32[2]{0:T(128)} %pad_add_fusion.place, s32[16,16]{1,0:T(8,128)} %choose.9, s32[16]{0:T(128)} %live.9, bf16[512,5120]{1,0:T(8,128)(2,1)} %queries.9, bf16[512,1024]{1,0:T(8,128)(2,1)} %keys.13, bf16[512,1024]{1,0:T(8,128)(2,1)} %values.13, ...), custom_call_target="tpu_custom_call", output_to_operand_aliasing={{}: (11, {})} | custom-call | flops 12000000000 | bytes 1048576 | tf_op jit(solution)/shard_map/attend/pallas_call | solution.py:423
  147.7 1.4 collective-permute-done.10.refs_2_
  149.1 5.1 %collective-permute-done.8.refs_1_ = bf16[4,2,128,128]{3,2,1,0:T(8,128)(2,1)} collective-permute-done((bf16[4,2,128,128]{3,2,1,0:T(8,128)(2,1)S(1)}, bf16[4,2,128,128]{3,2,1,0:T(8,128)(2,1)}, u32[]{:S(2)}, u32[]{:S(2)}) %collective-permute-start.8) | collective-permute-done | bytes 262176 | tf_op jit(solution)/shard_map/swap_3_1/ppermute | solution.py:461
  154.2 5.1 %attend.9 = bf16[512,5120]{1,0:T(8,128)(2,1)} custom-call(s32[2]{0:T(128)} %pad_add_fusion.place, s32[16,16]{1,0:T(8,128)} %choose.9, s32[16]{0:T(128)} %live.9, bf16[512,5120]{1,0:T(8,128)(2,1)} %queries.9, bf16[512,1024]{1,0:T(8,128)(2,1)} %keys.13, bf16[512,1024]{1,0:T(8,128)(2,1)} %values.13, ...), custom_call_target="tpu_custom_call", output_to_operand_aliasing={{}: (10, {})} | custom-call | flops 6000000000 | bytes 1048576 | tf_op jit(solution)/shard_map/attend/pallas_call | solution.py:423
  (22 shorter events, 0.1 us)
Async XLA Ops:
  0.0 5.5 %copy-start = (s32[16,16,2]{1,2,0:T(2,128)S(1)}, s32[16,16,2]{1,2,0:T(2,128)}, u32[]{:S(2)}) copy-start(s32[16,16,2]{1,2,0:T(2,128)} %param.9) | copy-start | bytes 6148
  1.0 10.3 %collective-permute-start = (bf16[2,512,128]{2,1,0:T(8,128)(2,1)S(1)}, bf16[2,512,128]{2,1,0:T(8,128)(2,1)}, u32[]{:S(2)}, u32[]{:S(2)}) collective-permute-start(bf16[2,512,128]{2,1,0:T(8,128)(2,1)S(1)} %pad_maximum_fusion.1), channel_id=1, source_target_pairs={{0,1},{1,0},{2,3},{3,2},{4,5},{5,4},{6,7},{7,6},{8,9},{9,8},{10,11... | collective-permute-start | bytes 786440 | tf_op jit(solution)/shard_map/other_plane_0/ppermute | solution.py:368
  5.4 22.0 %collective-permute-start.1 = (bf16[2,512,384]{2,1,0:T(8,128)(2,1)S(1)}, bf16[2,512,384]{2,1,0:T(8,128)(2,1)}, u32[]{:S(2)}, u32[]{:S(2)}) collective-permute-start(bf16[2,512,384]{2,1,0:T(8,128)(2,1)S(1)} %pad_maximum_fusion), channel_id=1, source_target_pairs={{0,1},{1,0},{2,3},{3,2},{4,5},{5,4},{6,7},{7,6},{8,9},{9,8},{10,11... | collective-permute-start | bytes 2359304 | tf_op jit(solution)/shard_map/other_plane_1/ppermute | solution.py:368
  14.5 29.2 %all-to-all-start = ((bf16[16,2,128,128]{3,2,1,0:T(8,128)(2,1)}), bf16[16,2,128,128]{3,2,1,0:T(8,128)(2,1)}, u32[]{:S(2)}, u32[]{:S(2)}) async-start(bf16[16,2,128,128]{3,2,1,0:T(8,128)(2,1)} %pick.2), calls=%async_computation | async-start | bytes 2097152 | tf_op jit(solution)/shard_map/shard_0/all_to_all | solution.py:476
  43.7 35.7 %all-to-all-start.1 = ((bf16[16,2,128,128]{3,2,1,0:T(8,128)(2,1)}), bf16[16,2,128,128]{3,2,1,0:T(8,128)(2,1)}, u32[]{:S(2)}, u32[]{:S(2)}) async-start(bf16[16,2,128,128]{3,2,1,0:T(8,128)(2,1)} %get-tuple-element.33), calls=%async_computation.1 | async-start | bytes 2097152 | tf_op jit(solution)/shard_map/shard_1/all_to_all | solution.py:476
  50.6 25.7 %collective-permute-start.5 = (bf16[1,16,2,128,128]{4,3,2,1,0:T(8,128)(2,1)}, bf16[1,16,2,128,128]{4,3,2,1,0:T(8,128)(2,1)}, u32[]{:S(2)}, u32[]{:S(2)}) collective-permute-start(bf16[1,16,2,128,128]{4,3,2,1,0:T(8,128)(2,1)} %bitcast.5.refs_0_), channel_id=1, source_target_pairs={{0,1},{1,0},{2,3},{3,2},{4,5},{5,4},{6,7},{7,6},{8,9},{9,8},{10,11... | collective-permute-start | bytes 3145736 | tf_op jit(solution)/shard_map/swap_0_0/ppermute | solution.py:461
  52.2 7.1 %collective-permute-start.2 = (bf16[4,2,128,128]{3,2,1,0:T(8,128)(2,1)}, bf16[4,2,128,128]{3,2,1,0:T(8,128)(2,1)S(1)}, u32[]{:S(2)}, u32[]{:S(2)}) collective-permute-start(bf16[4,2,128,128]{3,2,1,0:T(8,128)(2,1)} %get-tuple-element.28), channel_id=1, source_target_pairs={{0,2},{2,0},{4,6},{6,4},{8,10},{10,8},{12,14},{14,12},{16,18},{18,... | collective-permute-start | bytes 786440 | tf_op jit(solution)/shard_map/place_3_1/ppermute | solution.py:454
  52.2 16.0 %collective-permute-start.3 = (bf16[4,2,128,128]{3,2,1,0:T(8,128)(2,1)}, bf16[4,2,128,128]{3,2,1,0:T(8,128)(2,1)S(1)}, u32[]{:S(2)}, u32[]{:S(2)}) collective-permute-start(bf16[4,2,128,128]{3,2,1,0:T(8,128)(2,1)} %get-tuple-element.29), channel_id=1, source_target_pairs={{0,4},{2,6},{4,0},{6,2},{8,12},{10,14},{12,8},{14,10},{16,20},{18,... | collective-permute-start | bytes 786440 | tf_op jit(solution)/shard_map/place_3_2/ppermute | solution.py:454
  54.0 21.7 %collective-permute-start.4 = (bf16[4,2,128,128]{3,2,1,0:T(8,128)(2,1)}, bf16[4,2,128,128]{3,2,1,0:T(8,128)(2,1)S(1)}, u32[]{:S(2)}, u32[]{:S(2)}) collective-permute-start(bf16[4,2,128,128]{3,2,1,0:T(8,128)(2,1)} %get-tuple-element.30), channel_id=1, source_target_pairs={{0,6},{2,4},{4,2},{6,0},{8,14},{10,12},{12,10},{14,8},{16,22},{18,... | collective-permute-start | bytes 786440 | tf_op jit(solution)/shard_map/place_3_3/ppermute | solution.py:454
  59.3 17.1 %copy-start.1 = (bf16[4,2,128,128]{3,2,1,0:T(8,128)(2,1)}, bf16[4,2,128,128]{3,2,1,0:T(8,128)(2,1)S(1)}, u32[]{:S(2)}) copy-start(bf16[4,2,128,128]{3,2,1,0:T(8,128)(2,1)S(1)} %collective-permute-done.2.refs_1_) | copy-start | bytes 786436
  68.2 8.2 %copy-start.2 = (bf16[4,2,128,128]{3,2,1,0:T(8,128)(2,1)}, bf16[4,2,128,128]{3,2,1,0:T(8,128)(2,1)S(1)}, u32[]{:S(2)}) copy-start(bf16[4,2,128,128]{3,2,1,0:T(8,128)(2,1)S(1)} %collective-permute-done.3.refs_2_) | copy-start | bytes 786436
  75.7 0.7 copy-start.3
  79.4 28.5 %all-to-all-start.2 = ((bf16[16,2,128,128]{3,2,1,0:T(8,128)(2,1)}), bf16[16,2,128,128]{3,2,1,0:T(8,128)(2,1)}, u32[]{:S(2)}, u32[]{:S(2)}) async-start(bf16[16,2,128,128]{3,2,1,0:T(8,128)(2,1)} %get-tuple-element.41), calls=%async_computation.2 | async-start | bytes 2097152 | tf_op jit(solution)/shard_map/shard_2/all_to_all | solution.py:476
  84.9 31.9 %collective-permute-start.11 = (bf16[1,16,2,128,128]{4,3,2,1,0:T(8,128)(2,1)}, bf16[1,16,2,128,128]{4,3,2,1,0:T(8,128)(2,1)}, u32[]{:S(2)}, u32[]{:S(2)}) collective-permute-start(bf16[1,16,2,128,128]{4,3,2,1,0:T(8,128)(2,1)} %bitcast.8.refs_1_), channel_id=1, source_target_pairs={{0,1},{1,0},{2,3},{3,2},{4,5},{5,4},{6,7},{7,6},{8,9},{9,8},{10,11... | collective-permute-start | bytes 3145736 | tf_op jit(solution)/shard_map/swap_1_0/ppermute | solution.py:461
  86.5 30.3 %collective-permute-start.12 = (bf16[4,2,128,128]{3,2,1,0:T(8,128)(2,1)}, bf16[4,2,128,128]{3,2,1,0:T(8,128)(2,1)S(1)}, u32[]{:S(2)}, u32[]{:S(2)}) collective-permute-start(bf16[4,2,128,128]{3,2,1,0:T(8,128)(2,1)} %get-tuple-element.43.refs_3_), channel_id=1, source_target_pairs={{0,1},{1,0},{2,3},{3,2},{4,5},{5,4},{6,7},{7,6}} | collective-permute-start | bytes 786440 | tf_op jit(solution)/shard_map/swap_far/ppermute | solution.py:499
  96.4 32.6 %collective-permute-start.7 = (bf16[4,2,128,128]{3,2,1,0:T(8,128)(2,1)}, bf16[4,2,128,128]{3,2,1,0:T(8,128)(2,1)S(1)}, u32[]{:S(2)}, u32[]{:S(2)}) collective-permute-start(bf16[4,2,128,128]{3,2,1,0:T(8,128)(2,1)} %get-tuple-element.39), channel_id=1, source_target_pairs={{0,8},{2,10},{4,12},{6,14},{8,16},{10,18},{12,20},{14,22},{16,24},... | collective-permute-start | bytes 786440 | tf_op jit(solution)/shard_map/row_3_1/ppermute | solution.py:447
  99.5 29.1 %collective-permute-start.9 = (bf16[4,2,128,128]{3,2,1,0:T(8,128)(2,1)}, bf16[4,2,128,128]{3,2,1,0:T(8,128)(2,1)S(1)}, u32[]{:S(2)}, u32[]{:S(2)}) collective-permute-start(bf16[4,2,128,128]{3,2,1,0:T(8,128)(2,1)} %get-tuple-element.40), channel_id=1, source_target_pairs={{0,16},{2,18},{4,20},{6,22},{8,24},{10,26},{12,28},{14,30},{1,17},... | collective-permute-start | bytes 786440 | tf_op jit(solution)/shard_map/row_3_2/ppermute | solution.py:447
  107.9 32.2 %collective-permute-start.14 = (bf16[1,16,2,128,128]{4,3,2,1,0:T(8,128)(2,1)}, bf16[1,16,2,128,128]{4,3,2,1,0:T(8,128)(2,1)}, u32[]{:S(2)}, u32[]{:S(2)}) collective-permute-start(bf16[1,16,2,128,128]{4,3,2,1,0:T(8,128)(2,1)} %bitcast.9.refs_1_), channel_id=1, source_target_pairs={{0,1},{1,0},{2,3},{3,2},{4,5},{5,4},{6,7},{7,6},{8,9},{9,8},{10,11... | collective-permute-start | bytes 3145736 | tf_op jit(solution)/shard_map/swap_2_0/ppermute | solution.py:461
  116.8 0.7 copy-start.7
  125.0 8.1 %collective-permute-start.15 = (bf16[4,2,128,128]{3,2,1,0:T(8,128)(2,1)}, bf16[4,2,128,128]{3,2,1,0:T(8,128)(2,1)}, u32[]{:S(2)}, u32[]{:S(2)}) collective-permute-start(bf16[4,2,128,128]{3,2,1,0:T(8,128)(2,1)} %get-tuple-element.45), channel_id=1, source_target_pairs={{0,24},{2,26},{4,28},{6,30},{1,25},{3,27},{5,29},{7,31}} | collective-permute-start | bytes 786440 | tf_op jit(solution)/shard_map/row_3_3/ppermute | solution.py:447
  127.0 20.6 %collective-permute-start.6 = (bf16[3,2,128,128]{3,2,1,0:T(8,128)(2,1)}, bf16[3,2,128,128]{3,2,1,0:T(8,128)(2,1)}, u32[]{:S(2)}, u32[]{:S(2)}) collective-permute-start(bf16[3,2,128,128]{3,2,1,0:T(8,128)(2,1)} %get-tuple-element.38.refs_1_), channel_id=1, source_target_pairs={{0,1},{1,0},{2,3},{3,2},{4,5},{5,4},{6,7},{7,6},{8,9},{9,8},{10,11... | collective-permute-start | bytes 589832 | tf_op jit(solution)/shard_map/swap_3_0/ppermute | solution.py:461
  128.6 11.5 %copy-start.5 = (bf16[4,2,128,128]{3,2,1,0:T(8,128)(2,1)}, bf16[4,2,128,128]{3,2,1,0:T(8,128)(2,1)S(1)}, u32[]{:S(2)}) copy-start(bf16[4,2,128,128]{3,2,1,0:T(8,128)(2,1)S(1)} %collective-permute-done.9.refs_3_) | copy-start | bytes 786436
  128.6 20.5 %collective-permute-start.10 = (bf16[4,2,128,128]{3,2,1,0:T(8,128)(2,1)S(1)}, bf16[4,2,128,128]{3,2,1,0:T(8,128)(2,1)S(1)}, u32[]{:S(2)}, u32[]{:S(2)}) collective-permute-start(bf16[4,2,128,128]{3,2,1,0:T(8,128)(2,1)S(1)} %collective-permute-done.9.refs_3_), channel_id=1, source_target_pairs={{0,1},{1,0},{2,3},{3,2},{4,5},{5,4},{6,7},{7,6},{8,9},{9,8},{10,11... | collective-permute-start | bytes 786440 | tf_op jit(solution)/shard_map/swap_3_2/ppermute | solution.py:461
  129.1 11.0 %copy-start.4 = (bf16[4,2,128,128]{3,2,1,0:T(8,128)(2,1)}, bf16[4,2,128,128]{3,2,1,0:T(8,128)(2,1)S(1)}, u32[]{:S(2)}) copy-start(bf16[4,2,128,128]{3,2,1,0:T(8,128)(2,1)S(1)} %collective-permute-done.7.refs_2_) | copy-start | bytes 786436
  129.1 25.1 %collective-permute-start.8 = (bf16[4,2,128,128]{3,2,1,0:T(8,128)(2,1)S(1)}, bf16[4,2,128,128]{3,2,1,0:T(8,128)(2,1)}, u32[]{:S(2)}, u32[]{:S(2)}) collective-permute-start(bf16[4,2,128,128]{3,2,1,0:T(8,128)(2,1)S(1)} %collective-permute-done.7.refs_2_), channel_id=1, source_target_pairs={{0,1},{1,0},{2,3},{3,2},{4,5},{5,4},{6,7},{7,6},{8,9},{9,8},{10,11... | collective-permute-start | bytes 786440 | tf_op jit(solution)/shard_map/swap_3_1/ppermute | solution.py:461
  133.2 21.0 %collective-permute-start.13 = (bf16[4,2,128,128]{3,2,1,0:T(8,128)(2,1)}, bf16[4,2,128,128]{3,2,1,0:T(8,128)(2,1)}, u32[]{:S(2)}, u32[]{:S(2)}) collective-permute-start(bf16[4,2,128,128]{3,2,1,0:T(8,128)(2,1)} %get-tuple-element.44), channel_id=1, source_target_pairs={{0,24},{2,26},{4,28},{6,30},{1,25},{3,27},{5,29},{7,31}} | collective-permute-start | bytes 786440 | tf_op jit(solution)/shard_map/row_4_3/ppermute | solution.py:447
  149.1 5.1 %copy-start.6 = (bf16[4,2,128,128]{3,2,1,0:T(8,128)(2,1)}, bf16[4,2,128,128]{3,2,1,0:T(8,128)(2,1)S(1)}, u32[]{:S(2)}) copy-start(bf16[4,2,128,128]{3,2,1,0:T(8,128)(2,1)S(1)} %collective-permute-done.10.refs_2_) | copy-start | bytes 786436
where the time goes:
time: 162 us; the launch traced here: 159 us
  waiting for transfers between devices  60.3 us (37%)
  starting transfers between devices  50.6 us (31%)
  Pallas kernels  43.6 us (27%)
  local copies, waits for them, and re-layouts  3.85 us (2%)
    pallas_call x5, Pallas kernels, attend(): pl.pallas_call(functools.partial(attend_kernel, (n_seq, n_head, local_hea...  32.8 us
    all_to_all x3, starting transfers between devices, direct(): got = lax.all_to_all(sends, 'seq', split_axis=0, concat_axis=0, tiled=True)  18.6 us
    ppermute x3, waiting for transfers between devices, in_row(): lax.ppermute(arrays[m], 'seq', [(s, s ^ m) for s in range(n_seq)])  16.4 us
    ppermute x4, starting transfers between devices, over_rows(): got[ahead] = lax.ppermute(arrays[ahead], 'seq', pairs)  16.3 us
    all_to_all x3, waiting for transfers between devices, direct(): got = lax.all_to_all(sends, 'seq', split_axis=0, concat_axis=0, tiled=True)  15.7 us
    ppermute x2, waiting for transfers between devices, exchange(): others.append(lax.ppermute(part, 'head', back))  11.1 us
    ppermute x6, starting transfers between devices, swap(): got.append(lax.ppermute(array, 'head', [(0, 1), (1, 0)]))  8.23 us
    pallas_call x2, Pallas kernels, pick(): pl.pallas_call(functools.partial(pick_kernel, (n_head, n_seq, forms, toke...  7.8 us
  transfers between devices with their start and end apart: 19, of which 11 were waited for; matrix products, arithmetic and copies ran while one was open for 2% of the time, Pallas kernels for 24%

commit v1 on v0

--- a/solution.py
+++ b/solution.py
@@ -15,7 +15,7 @@
 STEP_BLOCKS = 4
 MASKED = -1e30
 NEAR = 4
-ATTEND_FLOPS = 6 * 10**9
+ATTEND_FLOPS = 10 * 10**9
 ROW_ORDER = (2, 1, 3)
 PICK_FLOPS = 5 * 10**9
 VMEM_BYTES = 63 * 2**20
@@ -410,6 +410,17 @@
         )(place, *parts, *passed)
         return list(outs[:n_out]), *outs[n_out:]
 
+    def relay(after, array):
+        return pl.pallas_call(
+            lambda *refs: None,
+            out_shape=jax.ShapeDtypeStruct(array.shape, array.dtype),
+            in_specs=[ANY, ANY],
+            out_specs=ANY,
+            input_output_aliases={1: 0},
+            compiler_params=pltpu.CompilerParams(vmem_limit_bytes=VMEM_BYTES),
+            name="relay",
+        )(after, array)
+
     def attend(jobs, *passed):
         operands = [place, choose, live, queries, keys, values]
         shapes = []
@@ -490,10 +501,11 @@
     first_turned = swap(first[1], 0)
     out, straight = attend([own(0, first)], None, parts[0])
     parts = [straight] + in_row(parts, 3)[1:]
-    grouped, third, *first_turned = regroup("place", "row", False, parts, third, *first_turned)
+    grouped, third = regroup("place", "row", False, parts, third)
+    third = relay(first_turned[0], third)
     third = direct(2, third)
     job = ("turn", 1, 0, "shard", first_turned)
-    out, *grouped[:-1] = attend([job, own(1, second)], out, *grouped[:-1])
+    out, *grouped[1:-1] = attend([job, own(1, second)], out, *grouped[1:-1])
     ends = [(i, i ^ 1) for i in range(NEAR * n_head)]
     with jax.named_scope("swap_far"):
         twin = lax.ppermute(grouped[-1], ("seq", "head"), ends)

time: 162 us -> 161 us (level); the launches traced: 159 us -> 160 us
    ppermute x6, waiting for transfers between devices: 7.2 us -> 17.8 us  [swap(): got.append(lax.ppermute(array, 'head', [(0, 1), (1, 0)]))]
    ppermute x1, waiting for transfers between devices: 7.36 us -> 0.01 us  [body(): twin = lax.ppermute(grouped[-1], ('seq', 'head'), ends)]
    all_to_all x3, waiting for transfers between devices: 15.7 us -> 13.5 us  [direct(): got = lax.all_to_all(sends, 'seq', split_axis=0, concat_axis=0, tiled=True)]
    ppermute x4, starting transfers between devices: 16.3 us -> 18.4 us  [over_rows(): got[ahead] = lax.ppermute(arrays[ahead], 'seq', pairs)]
where the time goes in v1:
time: 161 us; the launch traced here: 160 us
  waiting for transfers between devices  59.9 us (37%)
  starting transfers between devices  52.1 us (32%)
  Pallas kernels  43.7 us (27%)
  local copies, waits for them, and re-layouts  3.8 us (2%)
    pallas_call x5, Pallas kernels, attend(): pl.pallas_call(functools.partial(attend_kernel, (n_seq, n_head, local_hea...  32.8 us
    ppermute x4, starting transfers between devices, over_rows(): got[ahead] = lax.ppermute(arrays[ahead], 'seq', pairs)  18.4 us
    all_to_all x3, starting transfers between devices, direct(): got = lax.all_to_all(sends, 'seq', split_axis=0, concat_axis=0, tiled=True)  18 us
    ppermute x6, waiting for transfers between devices, swap(): got.append(lax.ppermute(array, 'head', [(0, 1), (1, 0)]))  17.8 us
    ppermute x3, waiting for transfers between devices, in_row(): lax.ppermute(arrays[m], 'seq', [(s, s ^ m) for s in range(n_seq)])  16.4 us
    all_to_all x3, waiting for transfers between devices, direct(): got = lax.all_to_all(sends, 'seq', split_axis=0, concat_axis=0, tiled=True)  13.5 us
    ppermute x2, waiting for transfers between devices, exchange(): others.append(lax.ppermute(part, 'head', back))  11.1 us
    pallas_call x2, Pallas kernels, pick(): pl.pallas_call(functools.partial(pick_kernel, (n_head, n_seq, forms, toke...  7.81 us
  transfers between devices with their start and end apart: 19, of which 11 were waited for; matrix products, arithmetic and copies ran while one was open for 2% of the time, Pallas kernels for 24%

profile of v1, /device:TPU:0, one launch (start us, length us, event | category | flops | bytes accessed | tf_op | source)
XLA Modules:
  0.0 160.4 jit_solution(4248869081723791449)
XLA Ops:
  0.0 1.0 dynamic-slice_bitcast_fusion.2
  1.0 3.0 %collective-permute-start = (bf16[2,512,128]{2,1,0:T(8,128)(2,1)S(1)}, bf16[2,512,128]{2,1,0:T(8,128)(2,1)}, u32[]{:S(2)}, u32[]{:S(2)}) collective-permute-start(bf16[2,512,128]{2,1,0:T(8,128)(2,1)S(1)} %pad_maximum_fusion.1), channel_id=1, source_target_pairs={{0,1},{1,0},{2,3},{3,2},{4,5},{5,4},{6,7},{7,6},{8,9},{9,8},{10,11... | collective-permute-start | bytes 786440 | tf_op jit(solution)/shard_map/other_plane_0/ppermute | solution.py:368
  4.1 1.2 dynamic-slice_bitcast_fusion
  5.3 0.1 pad_maximum_fusion
  5.4 0.1 collective-permute-start.1
  5.5 0.1 constant_dynamic-slice_fusion
  5.6 0.1 copy.18
  5.6 0.7 copy.19.wanted
  6.3 0.6 pad_add_fusion.place
  6.9 4.4 %collective-permute-done.refs_0_ = bf16[2,512,128]{2,1,0:T(8,128)(2,1)} collective-permute-done((bf16[2,512,128]{2,1,0:T(8,128)(2,1)S(1)}, bf16[2,512,128]{2,1,0:T(8,128)(2,1)}, u32[]{:S(2)}, u32[]{:S(2)}) %collective-permute-start) | collective-permute-done | bytes 262176 | tf_op jit(solution)/shard_map/other_plane_0/ppermute | solution.py:368
  11.3 3.1 %pick.2 = bf16[16,2,128,128]{3,2,1,0:T(8,128)(2,1)} custom-call(s32[2]{0:T(128)} %pad_add_fusion.place, s32[16,2]{1,0:T(8,128)} %copy.19.wanted, bf16[512,1024]{1,0:T(8,128)(2,1)} %keys.13, bf16[512,1024]{1,0:T(8,128)(2,1)} %values.13, bf16[2,512,128]{2,1,0:T(8,128)(2,1)} %collective-permute-done.refs_0_), custom_call_target="tpu_custom_call" | custom-call | flops 5000000000 | bytes 1048576 | tf_op jit(solution)/shard_map/pick/pallas_call | solution.py:378
  14.5 6.2 %all-to-all-start = ((bf16[16,2,128,128]{3,2,1,0:T(8,128)(2,1)}), bf16[16,2,128,128]{3,2,1,0:T(8,128)(2,1)}, u32[]{:S(2)}, u32[]{:S(2)}) async-start(bf16[16,2,128,128]{3,2,1,0:T(8,128)(2,1)} %pick.2), calls=%async_computation | async-start | bytes 2097152 | tf_op jit(solution)/shard_map/shard_0/all_to_all | solution.py:487
  20.7 6.7 %collective-permute-done.1.refs_0_ = bf16[2,512,384]{2,1,0:T(8,128)(2,1)} collective-permute-done((bf16[2,512,384]{2,1,0:T(8,128)(2,1)S(1)}, bf16[2,512,384]{2,1,0:T(8,128)(2,1)}, u32[]{:S(2)}, u32[]{:S(2)}) %collective-permute-start.1) | collective-permute-done | bytes 786464 | tf_op jit(solution)/shard_map/other_plane_1/ppermute | solution.py:368
  27.3 4.7 %pick.3 = (bf16[16,2,128,128]{3,2,1,0:T(8,128)(2,1)}, bf16[16,2,128,128]{3,2,1,0:T(8,128)(2,1)}, bf16[3,2,128,128]{3,2,1,0:T(8,128)(2,1)}, bf16[4,2,128,128]{3,2...) custom-call(s32[2]{0:T(128)} %pad_add_fusion.place, s32[16,2]{1,0:T(8,128)} %copy.19.wanted, ...), custom_call_target="tpu_custom_call" | custom-call | flops 15000000512 | bytes 1048576 | tf_op jit(solution)/shard_map/pick/pallas_call | solution.py:378
  32.0 11.6 %all-to-all-done = bf16[16,2,128,128]{3,2,1,0:T(8,128)(2,1)} async-done(((bf16[16,2,128,128]{3,2,1,0:T(8,128)(2,1)}), bf16[16,2,128,128]{3,2,1,0:T(8,128)(2,1)}, u32[]{:S(2)}, u32[]{:S(2)}) %all-to-all-start) | async-done | bytes 1048608 | tf_op jit(solution)/shard_map/shard_0/all_to_all | solution.py:487
  43.7 6.9 %all-to-all-start.1 = ((bf16[16,2,128,128]{3,2,1,0:T(8,128)(2,1)}), bf16[16,2,128,128]{3,2,1,0:T(8,128)(2,1)}, u32[]{:S(2)}, u32[]{:S(2)}) async-start(bf16[16,2,128,128]{3,2,1,0:T(8,128)(2,1)} %get-tuple-element.31), calls=%async_computation.1 | async-start | bytes 2097152 | tf_op jit(solution)/shard_map/shard_1/all_to_all | solution.py:487
  50.6 1.6 collective-permute-start.6
  52.2 0.0 collective-permute-start.2
  52.2 1.8 %collective-permute-start.3 = (bf16[4,2,128,128]{3,2,1,0:T(8,128)(2,1)}, bf16[4,2,128,128]{3,2,1,0:T(8,128)(2,1)S(1)}, u32[]{:S(2)}, u32[]{:S(2)}) collective-permute-start(bf16[4,2,128,128]{3,2,1,0:T(8,128)(2,1)} %get-tuple-element.27), channel_id=1, source_target_pairs={{0,4},{2,6},{4,0},{6,2},{8,12},{10,14},{12,8},{14,10},{16,20},{18,... | collective-permute-start | bytes 786440 | tf_op jit(solution)/shard_map/place_3_2/ppermute | solution.py:465
  54.0 0.1 collective-permute-start.4
  54.1 5.1 %attend.5 = (bf16[512,5120]{1,0:T(8,128)(2,1)}, bf16[3,2,128,128]{3,2,1,0:T(8,128)(2,1)}) custom-call(s32[2]{0:T(128)} %pad_add_fusion.place, s32[16,16]{1,0:T(8,128)} %choose.9, s32[16]{0:T(128)} %live.9, bf16[512,5120]{1,0:T(8,128)(2,1)} %queries.9, bf16[512,1024]{1,0:T(8,128)(2,1)} %keys.13, ...), custom_call_target="tpu_custom_call", output_to_operand_aliasing={{1}: (7, {})} | custom-call | flops 10000000000 | bytes 1048576 | tf_op jit(solution)/shard_map/attend/pallas_call | solution.py:434
  59.3 0.0 collective-permute-done.2.refs_1_
  59.3 8.9 %collective-permute-done.3.refs_2_ = bf16[4,2,128,128]{3,2,1,0:T(8,128)(2,1)S(1)} collective-permute-done((bf16[4,2,128,128]{3,2,1,0:T(8,128)(2,1)}, bf16[4,2,128,128]{3,2,1,0:T(8,128)(2,1)S(1)}, u32[]{:S(2)}, u32[]{:S(2)}) %collective-permute-start.3) | collective-permute-done | bytes 262176 | tf_op jit(solution)/shard_map/place_3_2/ppermute | solution.py:465
  68.2 7.5 %collective-permute-done.4.refs_3_ = bf16[4,2,128,128]{3,2,1,0:T(8,128)(2,1)S(1)} collective-permute-done((bf16[4,2,128,128]{3,2,1,0:T(8,128)(2,1)}, bf16[4,2,128,128]{3,2,1,0:T(8,128)(2,1)S(1)}, u32[]{:S(2)}, u32[]{:S(2)}) %collective-permute-start.4) | collective-permute-done | bytes 262176 | tf_op jit(solution)/shard_map/place_3_3/ppermute | solution.py:465
  75.7 0.7 copy-done.3
  76.4 3.0 %regroup.1 = (bf16[3,2,128,128]{3,2,1,0:T(8,128)(2,1)}, bf16[4,2,128,128]{3,2,1,0:T(8,128)(2,1)}, bf16[4,2,128,128]{3,2,1,0:T(8,128)(2,1)}, bf16[4,2,128,128]{3,2,1,0:T(8,128)(2,1)}, bf16[16,2,128,128]{3,2,1,0:T(8,128)(2,1)}) custom-call(s32[2]{0:T(128)} %pad_add_fusion.place, ...), custom_call_target="tpu_custom_call", output_to_operand_aliasing={{4}: (5, {})} | custom-call | tf_op jit(solution)/shard_map/regroup/pallas_call | solution.py:400
  79.4 0.0 collective-permute-done.6.refs_0_
  79.5 4.8 %all-to-all-start.2 = ((bf16[16,2,128,128]{3,2,1,0:T(8,128)(2,1)}), bf16[16,2,128,128]{3,2,1,0:T(8,128)(2,1)}, u32[]{:S(2)}, u32[]{:S(2)}) async-start(bf16[16,2,128,128]{3,2,1,0:T(8,128)(2,1)} %relay.1), calls=%async_computation.2 | async-start | bytes 2097152 | tf_op jit(solution)/shard_map/shard_2/all_to_all | solution.py:487
  84.3 3.4 %collective-permute-start.12 = (bf16[4,2,128,128]{3,2,1,0:T(8,128)(2,1)S(1)}, bf16[4,2,128,128]{3,2,1,0:T(8,128)(2,1)}, u32[]{:S(2)}, u32[]{:S(2)}) collective-permute-start(bf16[4,2,128,128]{3,2,1,0:T(8,128)(2,1)S(1)} %copy-done.6), channel_id=1, source_target_pairs={{0,1},{1,0},{2,3},{3,2},{4,5},{5,4},{6,7},{7,6}} | collective-permute-start | bytes 786440 | tf_op jit(solution)/shard_map/swap_far/ppermute | solution.py:511
  87.7 0.6 collective-permute-start.11
  88.3 7.5 %attend.6 = (bf16[512,5120]{1,0:T(8,128)(2,1)}, bf16[4,2,128,128]{3,2,1,0:T(8,128)(2,1)}, bf16[4,2,128,128]{3,2,1,0:T(8,128)(2,1)}) custom-call(s32[2]{0:T(128)} %pad_add_fusion.place, s32[16,16]{1,0:T(8,128)} %choose.9, s32[16]{0:T(128)} %live.9, bf16[512,5120]{1,0:T(8,128)(2,1)} %queries.9, ...), custom_call_target="tpu_custom_call", output_to_operand_aliasing={{0}: (8, {}), {1}: (9, {}), {2}: (10, {})} | custom-call | flops 20000000000 | bytes 1048576 | tf_op jit(solution)/shard_map/attend/pallas_call | solution.py:434
  95.8 5.6 %collective-permute-start.7 = (bf16[4,2,128,128]{3,2,1,0:T(8,128)(2,1)}, bf16[4,2,128,128]{3,2,1,0:T(8,128)(2,1)S(1)}, u32[]{:S(2)}, u32[]{:S(2)}) collective-permute-start(bf16[4,2,128,128]{3,2,1,0:T(8,128)(2,1)} %get-tuple-element.35), channel_id=1, source_target_pairs={{0,8},{2,10},{4,12},{6,14},{8,16},{10,18},{12,20},{14,22},{16,24},... | collective-permute-start | bytes 786440 | tf_op jit(solution)/shard_map/row_3_1/ppermute | solution.py:458
  101.4 4.0 %collective-permute-start.9 = (bf16[4,2,128,128]{3,2,1,0:T(8,128)(2,1)}, bf16[4,2,128,128]{3,2,1,0:T(8,128)(2,1)S(1)}, u32[]{:S(2)}, u32[]{:S(2)}) collective-permute-start(bf16[4,2,128,128]{3,2,1,0:T(8,128)(2,1)} %get-tuple-element.36), channel_id=1, source_target_pairs={{0,16},{2,18},{4,20},{6,22},{8,24},{10,26},{12,28},{14,30},{1,17},... | collective-permute-start | bytes 786440 | tf_op jit(solution)/shard_map/row_3_2/ppermute | solution.py:458
  105.4 1.9 %all-to-all-done.2 = bf16[16,2,128,128]{3,2,1,0:T(8,128)(2,1)} async-done(((bf16[16,2,128,128]{3,2,1,0:T(8,128)(2,1)}), bf16[16,2,128,128]{3,2,1,0:T(8,128)(2,1)}, u32[]{:S(2)}, u32[]{:S(2)}) %all-to-all-start.2) | async-done | bytes 1048608 | tf_op jit(solution)/shard_map/shard_2/all_to_all | solution.py:487
  107.3 1.5 collective-permute-start.14
  108.8 9.1 %collective-permute-done.11.refs_0_ = bf16[1,16,2,128,128]{4,3,2,1,0:T(8,128)(2,1)} collective-permute-done((bf16[1,16,2,128,128]{4,3,2,1,0:T(8,128)(2,1)}, bf16[1,16,2,128,128]{4,3,2,1,0:T(8,128)(2,1)}, u32[]{:S(2)}, u32[]{:S(2)}) %collective-permute-start.11) | collective-permute-done | bytes 1048608 | tf_op jit(solution)/shard_map/swap_1_0/ppermute | solution.py:472
  117.9 7.5 %attend.7 = (bf16[512,5120]{1,0:T(8,128)(2,1)}, bf16[4,2,128,128]{3,2,1,0:T(8,128)(2,1)}, bf16[4,2,128,128]{3,2,1,0:T(8,128)(2,1)}) custom-call(s32[2]{0:T(128)} %pad_add_fusion.place, s32[16,16]{1,0:T(8,128)} %choose.9, s32[16]{0:T(128)} %live.9, bf16[512,5120]{1,0:T(8,128)(2,1)} %queries.9, ...), custom_call_target="tpu_custom_call", output_to_operand_aliasing={{0}: (8, {}), {1}: (9, {}), {2}: (10, {})} | custom-call | flops 20000000000 | bytes 1048576 | tf_op jit(solution)/shard_map/attend/pallas_call | solution.py:434
  125.4 2.0 %collective-permute-start.15 = (bf16[4,2,128,128]{3,2,1,0:T(8,128)(2,1)}, bf16[4,2,128,128]{3,2,1,0:T(8,128)(2,1)}, u32[]{:S(2)}, u32[]{:S(2)}) collective-permute-start(bf16[4,2,128,128]{3,2,1,0:T(8,128)(2,1)} %get-tuple-element.41), channel_id=1, source_target_pairs={{0,24},{2,26},{4,28},{6,30},{1,25},{3,27},{5,29},{7,31}} | collective-permute-start | bytes 786440 | tf_op jit(solution)/shard_map/row_3_3/ppermute | solution.py:458
  127.4 1.5 collective-permute-start.5
  129.0 0.5 collective-permute-start.10
  129.5 1.5 collective-permute-start.8
  131.0 1.1 collective-permute-done.15.refs_4_
  132.0 6.9 %collective-permute-start.13 = (bf16[4,2,128,128]{3,2,1,0:T(8,128)(2,1)}, bf16[4,2,128,128]{3,2,1,0:T(8,128)(2,1)}, u32[]{:S(2)}, u32[]{:S(2)}) collective-permute-start(bf16[4,2,128,128]{3,2,1,0:T(8,128)(2,1)} %get-tuple-element.40), channel_id=1, source_target_pairs={{0,24},{2,26},{4,28},{6,30},{1,25},{3,27},{5,29},{7,31}} | collective-permute-start | bytes 786440 | tf_op jit(solution)/shard_map/row_4_3/ppermute | solution.py:458
  138.9 1.4 collective-permute-done.14.refs_0_
  140.4 7.6 %attend.8.refs_4_ = bf16[512,5120]{1,0:T(8,128)(2,1)} custom-call(s32[2]{0:T(128)} %pad_add_fusion.place, s32[16,16]{1,0:T(8,128)} %choose.9, s32[16]{0:T(128)} %live.9, bf16[512,5120]{1,0:T(8,128)(2,1)} %queries.9, bf16[512,1024]{1,0:T(8,128)(2,1)} %keys.13, bf16[512,1024]{1,0:T(8,128)(2,1)} %values.13, ...), custom_call_target="tpu_custom_call", output_to_operand_aliasing={{}: (11, {})} | custom-call | flops 20000000000 | bytes 1048576 | tf_op jit(solution)/shard_map/attend/pallas_call | solution.py:434
  148.0 2.1 %collective-permute-done.10.refs_2_ = bf16[4,2,128,128]{3,2,1,0:T(8,128)(2,1)S(1)} collective-permute-done((bf16[4,2,128,128]{3,2,1,0:T(8,128)(2,1)S(1)}, bf16[4,2,128,128]{3,2,1,0:T(8,128)(2,1)S(1)}, u32[]{:S(2)}, u32[]{:S(2)}) %collective-permute-start.10) | collective-permute-done | bytes 262176 | tf_op jit(solution)/shard_map/swap_3_2/ppermute | solution.py:472
  150.1 5.2 %collective-permute-done.8.refs_1_ = bf16[4,2,128,128]{3,2,1,0:T(8,128)(2,1)} collective-permute-done((bf16[4,2,128,128]{3,2,1,0:T(8,128)(2,1)S(1)}, bf16[4,2,128,128]{3,2,1,0:T(8,128)(2,1)}, u32[]{:S(2)}, u32[]{:S(2)}) %collective-permute-start.8) | collective-permute-done | bytes 262176 | tf_op jit(solution)/shard_map/swap_3_1/ppermute | solution.py:472
  155.3 5.1 %attend.9 = bf16[512,5120]{1,0:T(8,128)(2,1)} custom-call(s32[2]{0:T(128)} %pad_add_fusion.place, s32[16,16]{1,0:T(8,128)} %choose.9, s32[16]{0:T(128)} %live.9, bf16[512,5120]{1,0:T(8,128)(2,1)} %queries.9, bf16[512,1024]{1,0:T(8,128)(2,1)} %keys.13, bf16[512,1024]{1,0:T(8,128)(2,1)} %values.13, ...), custom_call_target="tpu_custom_call", output_to_operand_aliasing={{}: (10, {})} | custom-call | flops 10000000000 | bytes 1048576 | tf_op jit(solution)/shard_map/attend/pallas_call | solution.py:434
  (23 shorter events, 0.1 us)
Async XLA Ops:
  0.0 5.5 %copy-start = (s32[16,16,2]{1,2,0:T(2,128)S(1)}, s32[16,16,2]{1,2,0:T(2,128)}, u32[]{:S(2)}) copy-start(s32[16,16,2]{1,2,0:T(2,128)} %param.9) | copy-start | bytes 6148
  1.0 10.3 %collective-permute-start = (bf16[2,512,128]{2,1,0:T(8,128)(2,1)S(1)}, bf16[2,512,128]{2,1,0:T(8,128)(2,1)}, u32[]{:S(2)}, u32[]{:S(2)}) collective-permute-start(bf16[2,512,128]{2,1,0:T(8,128)(2,1)S(1)} %pad_maximum_fusion.1), channel_id=1, source_target_pairs={{0,1},{1,0},{2,3},{3,2},{4,5},{5,4},{6,7},{7,6},{8,9},{9,8},{10,11... | collective-permute-start | bytes 786440 | tf_op jit(solution)/shard_map/other_plane_0/ppermute | solution.py:368
  5.4 22.0 %collective-permute-start.1 = (bf16[2,512,384]{2,1,0:T(8,128)(2,1)S(1)}, bf16[2,512,384]{2,1,0:T(8,128)(2,1)}, u32[]{:S(2)}, u32[]{:S(2)}) collective-permute-start(bf16[2,512,384]{2,1,0:T(8,128)(2,1)S(1)} %pad_maximum_fusion), channel_id=1, source_target_pairs={{0,1},{1,0},{2,3},{3,2},{4,5},{5,4},{6,7},{7,6},{8,9},{9,8},{10,11... | collective-permute-start | bytes 2359304 | tf_op jit(solution)/shard_map/other_plane_1/ppermute | solution.py:368
  14.5 29.2 %all-to-all-start = ((bf16[16,2,128,128]{3,2,1,0:T(8,128)(2,1)}), bf16[16,2,128,128]{3,2,1,0:T(8,128)(2,1)}, u32[]{:S(2)}, u32[]{:S(2)}) async-start(bf16[16,2,128,128]{3,2,1,0:T(8,128)(2,1)} %pick.2), calls=%async_computation | async-start | bytes 2097152 | tf_op jit(solution)/shard_map/shard_0/all_to_all | solution.py:487
  43.7 35.8 %all-to-all-start.1 = ((bf16[16,2,128,128]{3,2,1,0:T(8,128)(2,1)}), bf16[16,2,128,128]{3,2,1,0:T(8,128)(2,1)}, u32[]{:S(2)}, u32[]{:S(2)}) async-start(bf16[16,2,128,128]{3,2,1,0:T(8,128)(2,1)} %get-tuple-element.31), calls=%async_computation.1 | async-start | bytes 2097152 | tf_op jit(solution)/shard_map/shard_1/all_to_all | solution.py:487
  50.6 28.8 %collective-permute-start.6 = (bf16[1,16,2,128,128]{4,3,2,1,0:T(8,128)(2,1)}, bf16[1,16,2,128,128]{4,3,2,1,0:T(8,128)(2,1)}, u32[]{:S(2)}, u32[]{:S(2)}) collective-permute-start(bf16[1,16,2,128,128]{4,3,2,1,0:T(8,128)(2,1)} %bitcast.5.refs_0_), channel_id=1, source_target_pairs={{0,1},{1,0},{2,3},{3,2},{4,5},{5,4},{6,7},{7,6},{8,9},{9,8},{10,11... | collective-permute-start | bytes 3145736 | tf_op jit(solution)/shard_map/swap_0_0/ppermute | solution.py:472
  52.2 7.1 %collective-permute-start.2 = (bf16[4,2,128,128]{3,2,1,0:T(8,128)(2,1)}, bf16[4,2,128,128]{3,2,1,0:T(8,128)(2,1)S(1)}, u32[]{:S(2)}, u32[]{:S(2)}) collective-permute-start(bf16[4,2,128,128]{3,2,1,0:T(8,128)(2,1)} %get-tuple-element.26), channel_id=1, source_target_pairs={{0,2},{2,0},{4,6},{6,4},{8,10},{10,8},{12,14},{14,12},{16,18},{18,... | collective-permute-start | bytes 786440 | tf_op jit(solution)/shard_map/place_3_1/ppermute | solution.py:465
  52.2 16.0 %collective-permute-start.3 = (bf16[4,2,128,128]{3,2,1,0:T(8,128)(2,1)}, bf16[4,2,128,128]{3,2,1,0:T(8,128)(2,1)S(1)}, u32[]{:S(2)}, u32[]{:S(2)}) collective-permute-start(bf16[4,2,128,128]{3,2,1,0:T(8,128)(2,1)} %get-tuple-element.27), channel_id=1, source_target_pairs={{0,4},{2,6},{4,0},{6,2},{8,12},{10,14},{12,8},{14,10},{16,20},{18,... | collective-permute-start | bytes 786440 | tf_op jit(solution)/shard_map/place_3_2/ppermute | solution.py:465
  54.0 21.7 %collective-permute-start.4 = (bf16[4,2,128,128]{3,2,1,0:T(8,128)(2,1)}, bf16[4,2,128,128]{3,2,1,0:T(8,128)(2,1)S(1)}, u32[]{:S(2)}, u32[]{:S(2)}) collective-permute-start(bf16[4,2,128,128]{3,2,1,0:T(8,128)(2,1)} %get-tuple-element.28), channel_id=1, source_target_pairs={{0,6},{2,4},{4,2},{6,0},{8,14},{10,12},{12,10},{14,8},{16,22},{18,... | collective-permute-start | bytes 786440 | tf_op jit(solution)/shard_map/place_3_3/ppermute | solution.py:465
  59.3 16.4 %copy-start.1 = (bf16[4,2,128,128]{3,2,1,0:T(8,128)(2,1)}, bf16[4,2,128,128]{3,2,1,0:T(8,128)(2,1)S(1)}, u32[]{:S(2)}) copy-start(bf16[4,2,128,128]{3,2,1,0:T(8,128)(2,1)S(1)} %collective-permute-done.2.refs_1_) | copy-start | bytes 786436
  68.2 7.5 %copy-start.2 = (bf16[4,2,128,128]{3,2,1,0:T(8,128)(2,1)}, bf16[4,2,128,128]{3,2,1,0:T(8,128)(2,1)S(1)}, u32[]{:S(2)}) copy-start(bf16[4,2,128,128]{3,2,1,0:T(8,128)(2,1)S(1)} %collective-permute-done.3.refs_2_) | copy-start | bytes 786436
  75.7 0.7 copy-start.3
  79.4 4.9 %copy-start.6 = (bf16[4,2,128,128]{3,2,1,0:T(8,128)(2,1)S(1)}, bf16[4,2,128,128]{3,2,1,0:T(8,128)(2,1)}, u32[]{:S(2)}) copy-start(bf16[4,2,128,128]{3,2,1,0:T(8,128)(2,1)} %get-tuple-element.39.refs_3_) | copy-start | bytes 786436
  79.5 27.8 %all-to-all-start.2 = ((bf16[16,2,128,128]{3,2,1,0:T(8,128)(2,1)}), bf16[16,2,128,128]{3,2,1,0:T(8,128)(2,1)}, u32[]{:S(2)}, u32[]{:S(2)}) async-start(bf16[16,2,128,128]{3,2,1,0:T(8,128)(2,1)} %relay.1), calls=%async_computation.2 | async-start | bytes 2097152 | tf_op jit(solution)/shard_map/shard_2/all_to_all | solution.py:487
  84.3 24.5 %collective-permute-start.12 = (bf16[4,2,128,128]{3,2,1,0:T(8,128)(2,1)S(1)}, bf16[4,2,128,128]{3,2,1,0:T(8,128)(2,1)}, u32[]{:S(2)}, u32[]{:S(2)}) collective-permute-start(bf16[4,2,128,128]{3,2,1,0:T(8,128)(2,1)S(1)} %copy-done.6), channel_id=1, source_target_pairs={{0,1},{1,0},{2,3},{3,2},{4,5},{5,4},{6,7},{7,6}} | collective-permute-start | bytes 786440 | tf_op jit(solution)/shard_map/swap_far/ppermute | solution.py:511
  87.7 30.2 %collective-permute-start.11 = (bf16[1,16,2,128,128]{4,3,2,1,0:T(8,128)(2,1)}, bf16[1,16,2,128,128]{4,3,2,1,0:T(8,128)(2,1)}, u32[]{:S(2)}, u32[]{:S(2)}) collective-permute-start(bf16[1,16,2,128,128]{4,3,2,1,0:T(8,128)(2,1)} %bitcast.8.refs_1_), channel_id=1, source_target_pairs={{0,1},{1,0},{2,3},{3,2},{4,5},{5,4},{6,7},{7,6},{8,9},{9,8},{10,11... | collective-permute-start | bytes 3145736 | tf_op jit(solution)/shard_map/swap_1_0/ppermute | solution.py:472
  95.8 33.7 %collective-permute-start.7 = (bf16[4,2,128,128]{3,2,1,0:T(8,128)(2,1)}, bf16[4,2,128,128]{3,2,1,0:T(8,128)(2,1)S(1)}, u32[]{:S(2)}, u32[]{:S(2)}) collective-permute-start(bf16[4,2,128,128]{3,2,1,0:T(8,128)(2,1)} %get-tuple-element.35), channel_id=1, source_target_pairs={{0,8},{2,10},{4,12},{6,14},{8,16},{10,18},{12,20},{14,22},{16,24},... | collective-permute-start | bytes 786440 | tf_op jit(solution)/shard_map/row_3_1/ppermute | solution.py:458
  101.4 27.5 %collective-permute-start.9 = (bf16[4,2,128,128]{3,2,1,0:T(8,128)(2,1)}, bf16[4,2,128,128]{3,2,1,0:T(8,128)(2,1)S(1)}, u32[]{:S(2)}, u32[]{:S(2)}) collective-permute-start(bf16[4,2,128,128]{3,2,1,0:T(8,128)(2,1)} %get-tuple-element.36), channel_id=1, source_target_pairs={{0,16},{2,18},{4,20},{6,22},{8,24},{10,26},{12,28},{14,30},{1,17},... | collective-permute-start | bytes 786440 | tf_op jit(solution)/shard_map/row_3_2/ppermute | solution.py:458
  107.3 33.1 %collective-permute-start.14 = (bf16[1,16,2,128,128]{4,3,2,1,0:T(8,128)(2,1)}, bf16[1,16,2,128,128]{4,3,2,1,0:T(8,128)(2,1)}, u32[]{:S(2)}, u32[]{:S(2)}) collective-permute-start(bf16[1,16,2,128,128]{4,3,2,1,0:T(8,128)(2,1)} %bitcast.9.refs_1_), channel_id=1, source_target_pairs={{0,1},{1,0},{2,3},{3,2},{4,5},{5,4},{6,7},{7,6},{8,9},{9,8},{10,11... | collective-permute-start | bytes 3145736 | tf_op jit(solution)/shard_map/swap_2_0/ppermute | solution.py:472
  125.4 6.6 %collective-permute-start.15 = (bf16[4,2,128,128]{3,2,1,0:T(8,128)(2,1)}, bf16[4,2,128,128]{3,2,1,0:T(8,128)(2,1)}, u32[]{:S(2)}, u32[]{:S(2)}) collective-permute-start(bf16[4,2,128,128]{3,2,1,0:T(8,128)(2,1)} %get-tuple-element.41), channel_id=1, source_target_pairs={{0,24},{2,26},{4,28},{6,30},{1,25},{3,27},{5,29},{7,31}} | collective-permute-start | bytes 786440 | tf_op jit(solution)/shard_map/row_3_3/ppermute | solution.py:458
  127.4 20.5 %collective-permute-start.5 = (bf16[3,2,128,128]{3,2,1,0:T(8,128)(2,1)}, bf16[3,2,128,128]{3,2,1,0:T(8,128)(2,1)}, u32[]{:S(2)}, u32[]{:S(2)}) collective-permute-start(bf16[3,2,128,128]{3,2,1,0:T(8,128)(2,1)} %get-tuple-element.30.refs_1_), channel_id=1, source_target_pairs={{0,1},{1,0},{2,3},{3,2},{4,5},{5,4},{6,7},{7,6},{8,9},{9,8},{10,11... | collective-permute-start | bytes 589832 | tf_op jit(solution)/shard_map/swap_3_0/ppermute | solution.py:472
  129.0 11.4 %copy-start.5 = (bf16[4,2,128,128]{3,2,1,0:T(8,128)(2,1)}, bf16[4,2,128,128]{3,2,1,0:T(8,128)(2,1)S(1)}, u32[]{:S(2)}) copy-start(bf16[4,2,128,128]{3,2,1,0:T(8,128)(2,1)S(1)} %collective-permute-done.9.refs_3_) | copy-start | bytes 786436
  129.0 21.1 %collective-permute-start.10 = (bf16[4,2,128,128]{3,2,1,0:T(8,128)(2,1)S(1)}, bf16[4,2,128,128]{3,2,1,0:T(8,128)(2,1)S(1)}, u32[]{:S(2)}, u32[]{:S(2)}) collective-permute-start(bf16[4,2,128,128]{3,2,1,0:T(8,128)(2,1)S(1)} %collective-permute-done.9.refs_3_), channel_id=1, source_target_pairs={{0,1},{1,0},{2,3},{3,2},{4,5},{5,4},{6,7},{7,6},{8,9},{9,8},{10,11... | collective-permute-start | bytes 786440 | tf_op jit(solution)/shard_map/swap_3_2/ppermute | solution.py:472
  129.5 10.9 %copy-start.4 = (bf16[4,2,128,128]{3,2,1,0:T(8,128)(2,1)}, bf16[4,2,128,128]{3,2,1,0:T(8,128)(2,1)S(1)}, u32[]{:S(2)}) copy-start(bf16[4,2,128,128]{3,2,1,0:T(8,128)(2,1)S(1)} %collective-permute-done.7.refs_2_) | copy-start | bytes 786436
  129.5 25.8 %collective-permute-start.8 = (bf16[4,2,128,128]{3,2,1,0:T(8,128)(2,1)S(1)}, bf16[4,2,128,128]{3,2,1,0:T(8,128)(2,1)}, u32[]{:S(2)}, u32[]{:S(2)}) collective-permute-start(bf16[4,2,128,128]{3,2,1,0:T(8,128)(2,1)S(1)} %collective-permute-done.7.refs_2_), channel_id=1, source_target_pairs={{0,1},{1,0},{2,3},{3,2},{4,5},{5,4},{6,7},{7,6},{8,9},{9,8},{10,11... | collective-permute-start | bytes 786440 | tf_op jit(solution)/shard_map/swap_3_1/ppermute | solution.py:472
  132.0 23.2 %collective-permute-start.13 = (bf16[4,2,128,128]{3,2,1,0:T(8,128)(2,1)}, bf16[4,2,128,128]{3,2,1,0:T(8,128)(2,1)}, u32[]{:S(2)}, u32[]{:S(2)}) collective-permute-start(bf16[4,2,128,128]{3,2,1,0:T(8,128)(2,1)} %get-tuple-element.40), channel_id=1, source_target_pairs={{0,24},{2,26},{4,28},{6,30},{1,25},{3,27},{5,29},{7,31}} | collective-permute-start | bytes 786440 | tf_op jit(solution)/shard_map/row_4_3/ppermute | solution.py:458
  150.1 5.2 %copy-start.7 = (bf16[4,2,128,128]{3,2,1,0:T(8,128)(2,1)}, bf16[4,2,128,128]{3,2,1,0:T(8,128)(2,1)S(1)}, u32[]{:S(2)}) copy-start(bf16[4,2,128,128]{3,2,1,0:T(8,128)(2,1)S(1)} %collective-permute-done.10.refs_2_) | copy-start | bytes 786436
